TPU v7x, 32 devices: a whole 2x2x4 slice. The times are simulated.
32 devices in a mesh: groups: 2 (over x), seq: 16 (over z, y, core).
Axes of the slice: x: 2, y: 2, z: 4, core: 2. Of those that a mesh axis runs over, the one named last changes fastest.
Arguments:
- dna_rows: bfloat16 [12, 1024, 768], P('groups', 'seq'), parts along dimension 0, may hold values from -6 to 6
- conv_weight: bfloat16 [5, 768, 768], replicated, may hold values from -0.09375 to 0.09375
- norm_gain: float32 [768], replicated, may hold values from 0.5 to 1.5
- w_query: bfloat16 [768, 768], replicated, may hold values from -3 to 3
- w_key: bfloat16 [768, 768], replicated, may hold values from -0.4375 to 0.4375
- w_value: bfloat16 [768, 768], replicated, may hold values from -0.21875 to 0.21875
- w_out: bfloat16 [768, 768], replicated, may hold values from -0.21875 to 0.21875
Outputs:
- pooled: bfloat16 [12, 512, 768], P('groups', 'seq'), parts along dimension 0
- attended: bfloat16 [12, 512, 768], P('groups', 'seq'), parts along dimension 0
There are 2 independent parts, one for each index of `groups`. A program takes and returns all parts, laid end to end along the dimension named above; an argument that names none is the same for every part. Nothing has to cross between parts.
All inputs are finite; a program needn't handle non-finite values.
Results may differ from a plain program's by a relative error of at most 0.038.
Values may be sent and summed in bfloat16 or wider, within the bound.
A program may use at most 128 MiB of HBM per device.

v0:
```python
import functools
import math

import jax
import jax.numpy as jnp
from jax import lax
from jax.experimental import pallas as pl
from jax.experimental.pallas import tpu as pltpu
from jax.sharding import PartitionSpec as P

HEADS = 8
TAPS = 5
DILATE = 2
LANES = 128
COLUMN_TILE = 256
MESH = pl.DeviceIdType.MESH


def kernel(
    n, seqs, rows,
    x_ref, conv_hbm, gain_ref, wq_hbm, wk_hbm, wv_hbm, wo_hbm,
    pooled_ref, attended_ref,
    conv_w, wq, wk, wv, wo,
    pad, taps, edge_out, edge_in, packed, got, mixed, back,
    conv_sem, w_sem, edge_send, edge_recv, pack_send, pack_recv, pack_local,
    back_send, back_recv, back_local,
):
    channels = x_ref.shape[-1]
    head = channels // HEADS
    half = rows // 2
    group = 2 * HEADS
    units = seqs // 2
    reach = 2 * DILATE
    pitch = rows + 2 * reach
    me = lax.axis_index("seq")
    mine = lax.rem(me, group)
    block = me - mine

    tiles = channels // COLUMN_TILE
    conv_copies = []
    for j in range(tiles):
        cols = pl.ds(j * COLUMN_TILE, COLUMN_TILE)
        conv_copies.append(
            pltpu.make_async_copy(conv_hbm.at[:, cols], conv_w.at[:, cols], conv_sem.at[j])
        )
    w_copies = [
        pltpu.make_async_copy(a, b, w_sem.at[i])
        for i, (a, b) in enumerate(((wq_hbm, wq), (wk_hbm, wk), (wv_hbm, wv), (wo_hbm, wo)))
    ]
    barrier = pltpu.get_barrier_semaphore()

    def greet(k, carry):
        pl.semaphore_signal(
            barrier, inc=1, device_id={"seq": lax.rem(me + k, n)}, device_id_type=MESH
        )
        return carry

    lax.fori_loop(1, n, greet, 0)
    for copy in conv_copies + w_copies:
        copy.start()

    for b in range(seqs):
        edge_out[0, b * reach : (b + 1) * reach, :] = x_ref[b, :8, :].astype(jnp.float32)[:reach]
        edge_out[1, b * reach : (b + 1) * reach, :] = x_ref[b, rows - 8 :, :].astype(jnp.float32)[
            8 - reach :
        ]
    pl.semaphore_wait(barrier, n - 1)

    def edge(side, target):
        return pltpu.make_async_remote_copy(
            src_ref=edge_out.at[side],
            dst_ref=edge_in.at[side],
            send_sem=edge_send.at[side],
            recv_sem=edge_recv.at[side],
            device_id={"seq": target},
            device_id_type=MESH,
        )

    to_left = edge(0, lax.rem(me + n - 1, n))
    to_right = edge(1, lax.rem(me + 1, n))
    to_left.start()
    to_right.start()
    strips = channels // LANES
    for b in range(seqs):
        for j in range(strips):
            strip = slice(j * LANES, (j + 1) * LANES)
            pad[j, b * pitch + reach : b * pitch + reach + rows, :] = x_ref[b, :, strip].astype(
                jnp.float32
            )
    to_left.wait()
    to_right.wait()
    has_left = jnp.where(me > 0, 1.0, 0.0).astype(jnp.float32)
    has_right = jnp.where(me < n - 1, 1.0, 0.0).astype(jnp.float32)
    for b in range(seqs):
        for j in range(strips):
            strip = slice(j * LANES, (j + 1) * LANES)
            pad[j, b * pitch : b * pitch + reach, :] = (
                edge_in[1, b * reach : (b + 1) * reach, strip] * has_left
            )
            pad[j, b * pitch + reach + rows : (b + 1) * pitch, :] = (
                edge_in[0, b * reach : (b + 1) * reach, strip] * has_right
            )

    for t in range(TAPS):
        for parity in range(2):
            for b in range(seqs):
                start = b * pitch + t * DILATE + parity
                to = (parity * seqs + b) * half
                for j in range(strips):
                    at = t * channels + j * LANES
                    taps[to : to + half, at : at + LANES] = (
                        pad[j, pl.ds(start, half, stride=2), :]
                    ).astype(jnp.bfloat16)

    count = seqs * half
    squares = jnp.zeros((count, 1), jnp.float32)
    middle = (TAPS // 2) * channels
    for j in range(tiles):
        conv_copies[j].wait()
        cols = slice(j * COLUMN_TILE, (j + 1) * COLUMN_TILE)
        conv_sum = jnp.dot(taps[...], conv_w[:, cols], preferred_element_type=jnp.float32)
        here = taps[:, middle + j * COLUMN_TILE : middle + (j + 1) * COLUMN_TILE]
        encoded = here.astype(jnp.float32) + jax.nn.gelu(conv_sum)
        pooled = ((encoded[:count] + encoded[count:]) * 0.5).astype(jnp.bfloat16)
        pooled_ref[:, cols] = pooled
        wide = pooled.astype(jnp.float32)
        squares = squares + jnp.sum(wide * wide, axis=-1, keepdims=True)
    shrink = lax.rsqrt(squares * (1.0 / channels) + 1e-06)
    normed = (pooled_ref[...].astype(jnp.float32) * shrink * gain_ref[...]).astype(jnp.bfloat16)

    projected = []
    for i, w in enumerate((wq, wk, wv)):
        w_copies[i].wait()
        projected.append(jnp.dot(normed, w[...], preferred_element_type=jnp.float32))

    width = packed.shape[-1]
    fill = jnp.zeros((half, width - 3 * units * head), jnp.float32)
    for g in range(group):
        h = g % HEADS
        pieces = []
        for c in range(units):
            b = 2 * c + g // HEADS
            for made in projected:
                pieces.append(made[b * half : (b + 1) * half, h * head : (h + 1) * head])
        packed[g] = jnp.concatenate(pieces + [fill], axis=-1).astype(jnp.bfloat16)

    bounds = [0] + [-(-3 * head * (c + 1) // LANES) * LANES for c in range(units)]
    parts = [pl.ds(bounds[c], bounds[c + 1] - bounds[c]) for c in range(units)]
    for c in range(units):
        pltpu.make_async_copy(
            packed.at[mine, :, parts[c]], got.at[me, :, parts[c]], pack_local.at[c]
        ).start()

        def scatter(k, carry, c=c):
            target = lax.rem(me + k, n)
            pltpu.make_async_remote_copy(
                src_ref=packed.at[lax.rem(target, group), :, parts[c]],
                dst_ref=got.at[me, :, parts[c]],
                send_sem=pack_send.at[c],
                recv_sem=pack_recv.at[c],
                device_id={"seq": target},
                device_id_type=MESH,
            ).start()
            return carry

        lax.fori_loop(1, n, scatter, 0)

    total = n * half
    queries = group * half
    step = 4 * half
    factor = math.log2(math.e) / math.sqrt(head)
    for c in range(units):
        pltpu.make_async_copy(
            packed.at[mine, :, parts[c]], got.at[me, :, parts[c]], pack_local.at[c]
        ).wait()
        others = got.at[pl.ds(0, n - 1), :, parts[c]]
        pltpu.make_async_copy(others, others, pack_recv.at[c]).wait()
        base = 3 * c * head
        keys = got[:, :, base + head : base + 2 * head].reshape(total, head)
        values = got[:, :, base + 2 * head : base + 3 * head].reshape(total, head)
        for q in range(queries // step):
            sources = step // half
            query = got[pl.ds(block + q * sources, sources), :, base : base + head].reshape(
                step, head
            )
            scores = lax.dot_general(
                query, keys, (((1,), (1,)), ((), ())), preferred_element_type=jnp.float32
            )
            top = jnp.max(scores, axis=-1, keepdims=True)
            terms = jnp.exp2((scores - top) * factor)
            row_sum = jnp.sum(terms, axis=-1, keepdims=True)
            out = jnp.dot(terms.astype(jnp.bfloat16), values, preferred_element_type=jnp.float32)
            out = (out / row_sum).astype(jnp.bfloat16)
            mixed[c, q * sources : (q + 1) * sources, :, :head] = out.reshape(sources, half, head)
        pltpu.make_async_copy(
            mixed.at[c, mine], back.at[c, mine], back_local.at[c]
        ).start()
        for k in range(1, group):
            index = lax.rem(mine + k, group)
            pltpu.make_async_remote_copy(
                src_ref=mixed.at[c, index],
                dst_ref=back.at[c, mine],
                send_sem=back_send.at[c],
                recv_sem=back_recv.at[c],
                device_id={"seq": block + index},
                device_id_type=MESH,
            ).start()

    w_copies[3].wait()
    for c in range(units):
        pltpu.make_async_copy(mixed.at[c, mine], back.at[c, mine], back_local.at[c]).wait()
        others = back.at[c, pl.ds(0, group - 1)]
        pltpu.make_async_copy(others, others, back_recv.at[c]).wait()
        attended = jnp.zeros((2 * half, channels), jnp.float32)
        for h in range(HEADS):
            both = jnp.concatenate(
                [back[c, h, :, :head], back[c, HEADS + h, :, :head]], axis=0
            )
            attended = attended + jnp.dot(
                both, wo[h * head : (h + 1) * head, :], preferred_element_type=jnp.float32
            )
        attended_ref[c * 2 * half : (c + 1) * 2 * half, :] = attended.astype(jnp.bfloat16)

    for c in range(units):
        others = got.at[pl.ds(0, n - 1), :, parts[c]]
        pltpu.make_async_copy(others, others, pack_send.at[c]).wait()
        others = back.at[c, pl.ds(0, group - 1)]
        pltpu.make_async_copy(others, others, back_send.at[c]).wait()


def on_device(dna_rows, conv_weight, norm_gain, w_query, w_key, w_value, w_out):
    n = lax.axis_size("seq")
    seqs, rows, channels = dna_rows.shape
    half = rows // 2
    group = 2 * HEADS
    units = seqs // 2
    head = channels // HEADS
    width = -(-3 * units * head // LANES) * LANES
    reach = 2 * DILATE
    bf16, f32 = jnp.bfloat16, jnp.float32
    vmem = pl.BlockSpec(memory_space=pltpu.VMEM)
    far = pl.BlockSpec(memory_space=pl.ANY)
    square = pltpu.VMEM((channels, channels), bf16)
    dma = pltpu.SemaphoreType.DMA
    pooled, attended = pl.pallas_call(
        functools.partial(kernel, n, seqs, rows),
        out_shape=[jax.ShapeDtypeStruct((seqs * half, channels), bf16)] * 2,
        in_specs=[vmem, far, vmem, far, far, far, far],
        out_specs=[vmem, vmem],
        scratch_shapes=[
            pltpu.VMEM((TAPS * channels, channels), bf16),
            square, square, square, square,
            pltpu.VMEM((channels // LANES, seqs * (rows + 2 * reach), LANES), f32),
            pltpu.VMEM((seqs * rows, TAPS * channels), bf16),
            pltpu.VMEM((2, seqs * reach, channels), f32),
            pltpu.VMEM((2, seqs * reach, channels), f32),
            pltpu.VMEM((group, half, width), bf16),
            pltpu.VMEM((n, half, width), bf16),
            pltpu.VMEM((units, group, half, LANES), bf16),
            pltpu.VMEM((units, group, half, LANES), bf16),
            dma((channels // COLUMN_TILE,)), dma((4,)),
            dma((2,)), dma((2,)),
            dma((units,)), dma((units,)), dma((units,)),
            dma((units,)), dma((units,)), dma((units,)),
        ],
        compiler_params=pltpu.CompilerParams(
            collective_id=0, has_side_effects=True, vmem_limit_bytes=56 * 1024 * 1024
        ),
    )(
        dna_rows,
        conv_weight.reshape(TAPS * channels, channels),
        norm_gain.reshape(1, channels),
        w_query, w_key, w_value, w_out,
    )
    return pooled.reshape(seqs, half, channels), attended.reshape(seqs, half, channels)


def solution(mesh):
    placed = (P("groups", "seq", None), P(), P(), P(), P(), P(), P())
    return jax.shard_map(
        on_device,
        mesh=mesh,
        in_specs=placed,
        out_specs=(P("groups", "seq", None), P("groups", "seq", None)),
        check_vma=False,
    )
```

profile of v0, /device:TPU:0, one launch (start us, length us, event | category | flops | bytes accessed | tf_op | source)
XLA Modules:
  0.0 55.7 jit_solution(106457897248064719)
XLA Ops:
  0.6 1.3 %reshape.17.gain_ref = f32[1,768]{1,0:T(1,128)} reshape(f32[768]{0:T(1024)} %param.9) | data formatting | bytes 6144 | tf_op jit(solution)/shard_map/reshape | solution.py:272
  1.9 50.4 %shard_map.86 = (bf16[192,768]{1,0:T(8,128)(2,1)}, bf16[192,768]{1,0:T(8,128)(2,1)}) custom-call(bf16[6,64,768]{2,1,0:T(8,128)(2,1)} %x_ref.1, bf16[3840,768]{1,0:T(8,128)(2,1)} %bitcast.3, f32[1,768]{1,0:T(1,128)} %reshape.17.gain_ref, bf16[768,768]{1,0:T(8,128)(2,1)} %wq_hbm.1, bf16[768,768]{1,0:T(8,128)(2,1)} %wk_hbm.1, bf16[768,768]{1,0:T(8,128)(2,1)} %wv_hbm.1, ...), custom_call_target="tpu_custom_call" | custom-call | tf_op jit(solution)/shard_map/pallas_call | solution.py:245
  52.3 1.7 %copy.11 = bf16[6,32,768]{2,1,0:T(8,128)(2,1)} copy(bf16[6,32,768]{2,1,0:T(8,128)(2,1)} %bitcast.5) | data formatting | bytes 589824
  54.0 1.7 %copy.12 = bf16[6,32,768]{2,1,0:T(8,128)(2,1)} copy(bf16[6,32,768]{2,1,0:T(8,128)(2,1)} %bitcast.4) | data formatting | bytes 589824
where the time goes:
time: 55.9 us; the launch traced here: 55.7 us
  Pallas kernels  50.4 us (90%)
  local copies, waits for them, and re-layouts  4.66 us (8%)
  between operations  0.64 us (1%)
    pallas_call x1, Pallas kernels, on_device(): pl.pallas_call(functools.partial(kernel, n, seqs, rows), out_shape=[jax.S...  50.4 us
    unnamed x2, local copies, waits for them, and re-layouts  3.39 us
    reshape x1, local copies, waits for them, and re-layouts, on_device(): norm_gain.reshape(1, channels)  1.27 us

commit v1 on v0

v1 whole, which is shorter than its diff:
```python
import functools
import math

import jax
import jax.numpy as jnp
from jax import lax
from jax.experimental import pallas as pl
from jax.experimental.pallas import tpu as pltpu
from jax.sharding import PartitionSpec as P

HEADS = 8
TAPS = 5
DILATE = 2
LANES = 128
COLUMN_TILE = 256
GROUP = 16
QUERY_ROWS = 256
MESH = pl.DeviceIdType.MESH


def kernel(
    n, seqs, rows,
    x_ref, conv_hbm, gain_ref, wq_hbm, wk_hbm, wv_hbm, wo_hbm,
    pooled_ref, attended_ref,
    conv_w, wq, wk, wv, wo,
    pad, taps, edge_out, edge_in, outgoing, got, q_rows, k_rows, v_rows, mixed, back,
    conv_sem, w_sem, edge_send, edge_recv, pack_sems, back_sems,
):
    channels = x_ref.shape[-1]
    head = channels // HEADS
    part = channels // 2
    half = rows // 2
    reach = 2 * DILATE
    slots = 2 * seqs
    idle = (GROUP - slots) // 2
    pitch = rows + 2 * reach
    me = lax.axis_index("seq")
    mine = lax.rem(me, GROUP)
    block = me - mine
    slot = mine - idle
    active = jnp.logical_and(slot >= 0, slot < slots)

    tiles = channels // COLUMN_TILE
    conv_copies = []
    for j in range(tiles):
        cols = pl.ds(j * COLUMN_TILE, COLUMN_TILE)
        conv_copies.append(
            pltpu.make_async_copy(conv_hbm.at[:, cols], conv_w.at[:, cols], conv_sem.at[j])
        )
    w_copies = [
        pltpu.make_async_copy(a, b, w_sem.at[i])
        for i, (a, b) in enumerate(((wq_hbm, wq), (wk_hbm, wk), (wv_hbm, wv), (wo_hbm, wo)))
    ]
    barrier = pltpu.get_barrier_semaphore()

    def greet(k, carry):
        pl.semaphore_signal(
            barrier, inc=1, device_id={"seq": lax.rem(me + k, n)}, device_id_type=MESH
        )
        return carry

    lax.fori_loop(1, n, greet, 0)
    for copy in conv_copies + w_copies:
        copy.start()

    for b in range(seqs):
        edge_out[0, b * reach : (b + 1) * reach, :] = x_ref[b, :8, :].astype(jnp.float32)[:reach]
        edge_out[1, b * reach : (b + 1) * reach, :] = x_ref[b, rows - 8 :, :].astype(jnp.float32)[
            8 - reach :
        ]
    pl.semaphore_wait(barrier, n - 1)

    def edge(side, target):
        return pltpu.make_async_remote_copy(
            src_ref=edge_out.at[side],
            dst_ref=edge_in.at[side],
            send_sem=edge_send.at[side],
            recv_sem=edge_recv.at[side],
            device_id={"seq": target},
            device_id_type=MESH,
        )

    to_left = edge(0, lax.rem(me + n - 1, n))
    to_right = edge(1, lax.rem(me + 1, n))
    to_left.start()
    to_right.start()
    strips = channels // LANES
    for b in range(seqs):
        for j in range(strips):
            strip = slice(j * LANES, (j + 1) * LANES)
            pad[j, b * pitch + reach : b * pitch + reach + rows, :] = x_ref[b, :, strip].astype(
                jnp.float32
            )
    to_left.wait()
    to_right.wait()
    has_left = jnp.where(me > 0, 1.0, 0.0).astype(jnp.float32)
    has_right = jnp.where(me < n - 1, 1.0, 0.0).astype(jnp.float32)
    for b in range(seqs):
        for j in range(strips):
            strip = slice(j * LANES, (j + 1) * LANES)
            pad[j, b * pitch : b * pitch + reach, :] = (
                edge_in[1, b * reach : (b + 1) * reach, strip] * has_left
            )
            pad[j, b * pitch + reach + rows : (b + 1) * pitch, :] = (
                edge_in[0, b * reach : (b + 1) * reach, strip] * has_right
            )

    for t in range(TAPS):
        for parity in range(2):
            for b in range(seqs):
                start = b * pitch + t * DILATE + parity
                to = (parity * seqs + b) * half
                for j in range(strips):
                    at = t * channels + j * LANES
                    taps[to : to + half, at : at + LANES] = (
                        pad[j, pl.ds(start, half, stride=2), :]
                    ).astype(jnp.bfloat16)

    count = seqs * half
    squares = jnp.zeros((count, 1), jnp.float32)
    middle = (TAPS // 2) * channels
    for j in range(tiles):
        conv_copies[j].wait()
        cols = slice(j * COLUMN_TILE, (j + 1) * COLUMN_TILE)
        conv_sum = jnp.dot(taps[...], conv_w[:, cols], preferred_element_type=jnp.float32)
        here = taps[:, middle + j * COLUMN_TILE : middle + (j + 1) * COLUMN_TILE]
        encoded = here.astype(jnp.float32) + jax.nn.gelu(conv_sum)
        pooled = ((encoded[:count] + encoded[count:]) * 0.5).astype(jnp.bfloat16)
        pooled_ref[:, cols] = pooled
        wide = pooled.astype(jnp.float32)
        squares = squares + jnp.sum(wide * wide, axis=-1, keepdims=True)
    shrink = lax.rsqrt(squares * (1.0 / channels) + 1e-06)
    normed = (pooled_ref[...].astype(jnp.float32) * shrink * gain_ref[...]).astype(jnp.bfloat16)

    for b in range(seqs):
        outgoing[b] = normed[b * half : (b + 1) * half]

    sends = slots * (n // GROUP)
    pack_send, pack_recv, pack_local = (pack_sems.at[i] for i in range(3))
    back_send, back_recv, back_local = (back_sems.at[i] for i in range(3))
    window = jnp.clip(slot, 0, slots - 1) // 2
    lanes = pl.ds(pl.multiple_of(lax.rem(jnp.clip(slot, 0, slots - 1), 2) * part, LANES), part)
    own = pltpu.make_async_copy(outgoing.at[window], got.at[me], pack_local)

    @pl.when(active)
    def _():
        own.start()

    def scatter(k, carry):
        to = lax.rem(k + mine, slots)
        target = (k // slots) * GROUP + idle + to

        @pl.when(target != me)
        def _():
            pltpu.make_async_remote_copy(
                src_ref=outgoing.at[to // 2],
                dst_ref=got.at[me],
                send_sem=pack_send,
                recv_sem=pack_recv,
                device_id={"seq": target},
                device_id_type=MESH,
            ).start()

        return carry

    lax.fori_loop(0, sends, scatter, 0)
    for copy in w_copies:
        copy.wait()

    def settle(ref, count, sem):
        some = ref.at[pl.ds(0, count)]
        pltpu.make_async_copy(some, some, sem).wait()

    kept = pltpu.make_async_copy(mixed.at[mine], back.at[jnp.clip(slot, 0, slots - 1)], back_local)
    factor = math.log2(math.e) / math.sqrt(head)

    @pl.when(active)
    def _():
        own.wait()
        settle(got, n - 1, pack_recv)

        def project(i, carry):
            made = got[pl.ds(i * GROUP, GROUP)].reshape(GROUP * half, channels)
            at = pl.ds(pl.multiple_of(i * (GROUP * half), GROUP * half), GROUP * half)
            k_rows[at, :] = jnp.dot(
                made, wk[:, lanes], preferred_element_type=jnp.float32
            ).astype(jnp.bfloat16)
            v_rows[at, :] = jnp.dot(
                made, wv[:, lanes], preferred_element_type=jnp.float32
            ).astype(jnp.bfloat16)
            return carry

        lax.fori_loop(0, n // GROUP, project, 0)
        asking = got[pl.ds(block, GROUP)].reshape(GROUP * half, channels)
        q_rows[...] = jnp.dot(
            asking, wq[:, lanes], preferred_element_type=jnp.float32
        ).astype(jnp.bfloat16)
        sources = QUERY_ROWS // half
        for q in range(GROUP // sources):
            outs = []
            for h in range(HEADS // 2):
                of_head = slice(h * head, (h + 1) * head)
                scores = lax.dot_general(
                    q_rows[q * QUERY_ROWS : (q + 1) * QUERY_ROWS, of_head],
                    k_rows[:, of_head],
                    (((1,), (1,)), ((), ())),
                    preferred_element_type=jnp.float32,
                )
                top = jnp.max(scores, axis=-1, keepdims=True)
                terms = jnp.exp2((scores - top) * factor)
                row_sum = jnp.sum(terms, axis=-1, keepdims=True)
                out = jnp.dot(
                    terms.astype(jnp.bfloat16),
                    v_rows[:, of_head],
                    preferred_element_type=jnp.float32,
                )
                outs.append(out / row_sum)
            joined = jnp.concatenate(outs, axis=-1).astype(jnp.bfloat16)
            mixed[q * sources : (q + 1) * sources] = joined.reshape(sources, half, part)
            for k in range(q * sources, (q + 1) * sources):

                @pl.when(mine != k)
                def _(k=k):
                    pltpu.make_async_remote_copy(
                        src_ref=mixed.at[k],
                        dst_ref=back.at[slot],
                        send_sem=back_send,
                        recv_sem=back_recv,
                        device_id={"seq": block + k},
                        device_id_type=MESH,
                    ).start()

                @pl.when(mine == k)
                def _():
                    kept.start()

        kept.wait()
        settle(back, slots - 1, back_recv)
        settle(mixed, GROUP - 1, back_send)
        settle(got, sends - 1, pack_send)

    @pl.when(jnp.logical_not(active))
    def _():
        settle(back, slots, back_recv)
        settle(got, sends, pack_send)

    attended = jnp.zeros((count, channels), jnp.float32)
    for i in range(2):
        joined = jnp.concatenate([back[2 * b + i] for b in range(seqs)], axis=0)
        attended = attended + jnp.dot(
            joined, wo[i * part : (i + 1) * part, :], preferred_element_type=jnp.float32
        )
    attended_ref[...] = attended.astype(jnp.bfloat16)


def on_device(dna_rows, conv_weight, norm_gain, w_query, w_key, w_value, w_out):
    n = lax.axis_size("seq")
    seqs, rows, channels = dna_rows.shape
    half = rows // 2
    part = channels // 2
    reach = 2 * DILATE
    bf16, f32 = jnp.bfloat16, jnp.float32
    vmem = pl.BlockSpec(memory_space=pltpu.VMEM)
    far = pl.BlockSpec(memory_space=pl.ANY)
    square = pltpu.VMEM((channels, channels), bf16)
    dma = pltpu.SemaphoreType.DMA
    pooled, attended = pl.pallas_call(
        functools.partial(kernel, n, seqs, rows),
        out_shape=[jax.ShapeDtypeStruct((seqs * half, channels), bf16)] * 2,
        in_specs=[vmem, far, vmem, far, far, far, far],
        out_specs=[vmem, vmem],
        scratch_shapes=[
            pltpu.VMEM((TAPS * channels, channels), bf16),
            square, square, square, square,
            pltpu.VMEM((channels // LANES, seqs * (rows + 2 * reach), LANES), f32),
            pltpu.VMEM((seqs * rows, TAPS * channels), bf16),
            pltpu.VMEM((2, seqs * reach, channels), f32),
            pltpu.VMEM((2, seqs * reach, channels), f32),
            pltpu.VMEM((seqs, half, channels), bf16),
            pltpu.VMEM((n, half, channels), bf16),
            pltpu.VMEM((GROUP * half, part), bf16),
            pltpu.VMEM((n * half, part), bf16),
            pltpu.VMEM((n * half, part), bf16),
            pltpu.VMEM((GROUP, half, part), bf16),
            pltpu.VMEM((2 * seqs, half, part), bf16),
            dma((channels // COLUMN_TILE,)), dma((4,)),
            dma((2,)), dma((2,)),
            dma((3,)), dma((3,)),
        ],
        compiler_params=pltpu.CompilerParams(
            collective_id=0, has_side_effects=True, vmem_limit_bytes=56 * 1024 * 1024
        ),
    )(
        dna_rows,
        conv_weight.reshape(TAPS * channels, channels),
        norm_gain.reshape(1, channels),
        w_query, w_key, w_value, w_out,
    )
    return pooled.reshape(seqs, half, channels), attended.reshape(seqs, half, channels)


def solution(mesh):
    placed = (P("groups", "seq", None), P(), P(), P(), P(), P(), P())
    return jax.shard_map(
        on_device,
        mesh=mesh,
        in_specs=placed,
        out_specs=(P("groups", "seq", None), P("groups", "seq", None)),
        check_vma=False,
    )
```

time: 55.9 us -> 47 us (0.84)
  the two profiles are of different devices: /device:TPU:0 before, /device:TPU:31 now
where the time goes in v1:
time: 47 us; the launch traced here: 46.7 us
  Pallas kernels  41.4 us (88%)
  local copies, waits for them, and re-layouts  4.66 us (10%)
  between operations  0.64 us (1%)
    pallas_call x1, Pallas kernels, on_device(): pl.pallas_call(functools.partial(kernel, n, seqs, rows), out_shape=[jax.S...  41.4 us
    unnamed x2, local copies, waits for them, and re-layouts  3.39 us
    reshape x1, local copies, waits for them, and re-layouts, on_device(): norm_gain.reshape(1, channels)  1.27 us

profile of v1, /device:TPU:31, one launch (start us, length us, event | category | flops | bytes accessed | tf_op | source)
XLA Modules:
  0.0 46.7 jit_solution(18125066411159227204)
XLA Ops:
  0.6 1.3 %reshape.17.gain_ref = f32[1,768]{1,0:T(1,128)} reshape(f32[768]{0:T(1024)} %param.9) | data formatting | bytes 6144 | tf_op jit(solution)/shard_map/reshape | solution.py:296
  1.9 41.4 %shard_map.86 = (bf16[192,768]{1,0:T(8,128)(2,1)}, bf16[192,768]{1,0:T(8,128)(2,1)}) custom-call(bf16[6,64,768]{2,1,0:T(8,128)(2,1)} %x_ref.1, bf16[3840,768]{1,0:T(8,128)(2,1)} %bitcast.3, f32[1,768]{1,0:T(1,128)} %reshape.17.gain_ref, bf16[768,768]{1,0:T(8,128)(2,1)} %wq_hbm.1, bf16[768,768]{1,0:T(8,128)(2,1)} %wk_hbm.1, bf16[768,768]{1,0:T(8,128)(2,1)} %wv_hbm.1, ...), custom_call_target="tpu_custom_call" | custom-call | tf_op jit(solution)/shard_map/pallas_call | solution.py:267
  43.3 1.7 %copy.11 = bf16[6,32,768]{2,1,0:T(8,128)(2,1)} copy(bf16[6,32,768]{2,1,0:T(8,128)(2,1)} %bitcast.5) | data formatting | bytes 589824
  45.0 1.7 %copy.12 = bf16[6,32,768]{2,1,0:T(8,128)(2,1)} copy(bf16[6,32,768]{2,1,0:T(8,128)(2,1)} %bitcast.4) | data formatting | bytes 589824

commit v2 on v1

--- a/solution.py
+++ b/solution.py
@@ -24,7 +24,7 @@
     pooled_ref, attended_ref,
     conv_w, wq, wk, wv, wo,
     pad, taps, edge_out, edge_in, outgoing, got, q_rows, k_rows, v_rows, mixed, back,
-    conv_sem, w_sem, edge_send, edge_recv, pack_sems, back_sems,
+    conv_sem, w_sem, edge_send, edge_recv, pack_sems, back_sems, twin_sems,
 ):
     channels = x_ref.shape[-1]
     head = channels // HEADS
@@ -130,12 +130,14 @@
         wide = pooled.astype(jnp.float32)
         squares = squares + jnp.sum(wide * wide, axis=-1, keepdims=True)
     shrink = lax.rsqrt(squares * (1.0 / channels) + 1e-06)
-    normed = (pooled_ref[...].astype(jnp.float32) * shrink * gain_ref[...]).astype(jnp.bfloat16)
+    normed = (pooled_ref[...].astype(jnp.float32) * shrink * gain_ref[...].reshape(1, channels)).astype(jnp.bfloat16)
 
     for b in range(seqs):
         outgoing[b] = normed[b * half : (b + 1) * half]
 
-    sends = slots * (n // GROUP)
+    sends = seqs * (n // GROUP)
+    core = lax.rem(me, 2)
+    twin = me + 1 - 2 * core
     pack_send, pack_recv, pack_local = (pack_sems.at[i] for i in range(3))
     back_send, back_recv, back_local = (back_sems.at[i] for i in range(3))
     window = jnp.clip(slot, 0, slots - 1) // 2
@@ -147,13 +149,13 @@
         own.start()
 
     def scatter(k, carry):
-        to = lax.rem(k + mine, slots)
-        target = (k // slots) * GROUP + idle + to
+        to = lax.rem(k + mine // 2, seqs)
+        target = (k // seqs) * GROUP + idle + 2 * to + core
 
         @pl.when(target != me)
         def _():
             pltpu.make_async_remote_copy(
-                src_ref=outgoing.at[to // 2],
+                src_ref=outgoing.at[to],
                 dst_ref=got.at[me],
                 send_sem=pack_send,
                 recv_sem=pack_recv,
@@ -177,7 +179,21 @@
     @pl.when(active)
     def _():
         own.wait()
-        settle(got, n - 1, pack_recv)
+        settle(got, n // 2 - 1, pack_recv)
+
+        def relay(i, carry):
+            pltpu.make_async_remote_copy(
+                src_ref=got.at[2 * i + core],
+                dst_ref=got.at[2 * i + core],
+                send_sem=twin_sems.at[0],
+                recv_sem=twin_sems.at[1],
+                device_id={"seq": twin},
+                device_id_type=MESH,
+            ).start()
+            return carry
+
+        lax.fori_loop(0, n // 2, relay, 0)
+        settle(got, n // 2, twin_sems.at[1])
 
         def project(i, carry):
             made = got[pl.ds(i * GROUP, GROUP)].reshape(GROUP * half, channels)
@@ -237,6 +253,7 @@
         kept.wait()
         settle(back, slots - 1, back_recv)
         settle(mixed, GROUP - 1, back_send)
+        settle(got, n // 2, twin_sems.at[0])
         settle(got, sends - 1, pack_send)
 
     @pl.when(jnp.logical_not(active))
@@ -285,7 +302,7 @@
             pltpu.VMEM((2 * seqs, half, part), bf16),
             dma((channels // COLUMN_TILE,)), dma((4,)),
             dma((2,)), dma((2,)),
-            dma((3,)), dma((3,)),
+            dma((3,)), dma((3,)), dma((2,)),
         ],
         compiler_params=pltpu.CompilerParams(
             collective_id=0, has_side_effects=True, vmem_limit_bytes=56 * 1024 * 1024
@@ -293,7 +310,7 @@
     )(
         dna_rows,
         conv_weight.reshape(TAPS * channels, channels),
-        norm_gain.reshape(1, channels),
+        norm_gain,
         w_query, w_key, w_value, w_out,
     )
     return pooled.reshape(seqs, half, channels), attended.reshape(seqs, half, channels)

time: 47 us -> 41.9 us (0.89)
  Pallas kernels: 41.4 us -> 37.7 us
  local copies, waits for them, and re-layouts: 4.66 us -> 3.39 us
    pallas_call x1, Pallas kernels: 41.4 us -> 37.7 us  [on_device(): pl.pallas_call(functools.partial(kernel, n, seqs, rows), out_shape=[jax.S...]
    reshape x1 -> x0, local copies, waits for them, and re-layouts: 1.27 us -> none  [on_device(): norm_gain.reshape(1, channels)]
where the time goes in v2:
time: 41.9 us; the launch traced here: 41.7 us
  Pallas kernels  37.7 us (90%)
  local copies, waits for them, and re-layouts  3.39 us (8%)
  between operations  0.64 us (2%)
    pallas_call x1, Pallas kernels, on_device(): pl.pallas_call(functools.partial(kernel, n, seqs, rows), out_shape=[jax.S...  37.7 us
    unnamed x2, local copies, waits for them, and re-layouts  3.39 us

profile of v2, /device:TPU:31, one launch (start us, length us, event | category | flops | bytes accessed | tf_op | source)
XLA Modules:
  0.0 41.7 jit_solution(8316741394022088938)
XLA Ops:
  0.6 37.7 %shard_map.86 = (bf16[192,768]{1,0:T(8,128)(2,1)}, bf16[192,768]{1,0:T(8,128)(2,1)}) custom-call(bf16[6,64,768]{2,1,0:T(8,128)(2,1)} %x_ref.1, bf16[3840,768]{1,0:T(8,128)(2,1)} %bitcast.3, f32[768]{0:T(1024)} %gain_ref.1, bf16[768,768]{1,0:T(8,128)(2,1)} %wq_hbm.1, bf16[768,768]{1,0:T(8,128)(2,1)} %wk_hbm.1, bf16[768,768]{1,0:T(8,128)(2,1)} %wv_hbm.1, ...), custom_call_target="tpu_custom_call" | custom-call | tf_op jit(solution)/shard_map/pallas_call | solution.py:284
  38.3 1.7 %copy.11 = bf16[6,32,768]{2,1,0:T(8,128)(2,1)} copy(bf16[6,32,768]{2,1,0:T(8,128)(2,1)} %bitcast.5) | data formatting | bytes 589824
  40.0 1.7 %copy.12 = bf16[6,32,768]{2,1,0:T(8,128)(2,1)} copy(bf16[6,32,768]{2,1,0:T(8,128)(2,1)} %bitcast.4) | data formatting | bytes 589824

commit v3 on v2

--- a/solution.py
+++ b/solution.py
@@ -14,6 +14,7 @@
 LANES = 128
 COLUMN_TILE = 256
 GROUP = 16
+STAGES = 3
 QUERY_ROWS = 256
 MESH = pl.DeviceIdType.MESH
 
@@ -105,36 +106,6 @@
                 edge_in[0, b * reach : (b + 1) * reach, strip] * has_right
             )
 
-    for t in range(TAPS):
-        for parity in range(2):
-            for b in range(seqs):
-                start = b * pitch + t * DILATE + parity
-                to = (parity * seqs + b) * half
-                for j in range(strips):
-                    at = t * channels + j * LANES
-                    taps[to : to + half, at : at + LANES] = (
-                        pad[j, pl.ds(start, half, stride=2), :]
-                    ).astype(jnp.bfloat16)
-
-    count = seqs * half
-    squares = jnp.zeros((count, 1), jnp.float32)
-    middle = (TAPS // 2) * channels
-    for j in range(tiles):
-        conv_copies[j].wait()
-        cols = slice(j * COLUMN_TILE, (j + 1) * COLUMN_TILE)
-        conv_sum = jnp.dot(taps[...], conv_w[:, cols], preferred_element_type=jnp.float32)
-        here = taps[:, middle + j * COLUMN_TILE : middle + (j + 1) * COLUMN_TILE]
-        encoded = here.astype(jnp.float32) + jax.nn.gelu(conv_sum)
-        pooled = ((encoded[:count] + encoded[count:]) * 0.5).astype(jnp.bfloat16)
-        pooled_ref[:, cols] = pooled
-        wide = pooled.astype(jnp.float32)
-        squares = squares + jnp.sum(wide * wide, axis=-1, keepdims=True)
-    shrink = lax.rsqrt(squares * (1.0 / channels) + 1e-06)
-    normed = (pooled_ref[...].astype(jnp.float32) * shrink * gain_ref[...].reshape(1, channels)).astype(jnp.bfloat16)
-
-    for b in range(seqs):
-        outgoing[b] = normed[b * half : (b + 1) * half]
-
     sends = seqs * (n // GROUP)
     core = lax.rem(me, 2)
     twin = me + 1 - 2 * core
@@ -144,28 +115,65 @@
     lanes = pl.ds(pl.multiple_of(lax.rem(jnp.clip(slot, 0, slots - 1), 2) * part, LANES), part)
     own = pltpu.make_async_copy(outgoing.at[window], got.at[me], pack_local)
 
-    @pl.when(active)
-    def _():
-        own.start()
-
-    def scatter(k, carry):
-        to = lax.rem(k + mine // 2, seqs)
-        target = (k // seqs) * GROUP + idle + 2 * to + core
-
-        @pl.when(target != me)
+    count = seqs * half
+    middle = (TAPS // 2) * channels
+    stage = seqs // STAGES
+    for p in range(STAGES):
+        first = 2 * p * stage * half
+        for t in range(TAPS):
+            for parity in range(2):
+                for b in range(stage):
+                    start = (p * stage + b) * pitch + t * DILATE + parity
+                    to = first + (parity * stage + b) * half
+                    for j in range(strips):
+                        at = t * channels + j * LANES
+                        taps[to : to + half, at : at + LANES] = (
+                            pad[j, pl.ds(start, half, stride=2), :]
+                        ).astype(jnp.bfloat16)
+        some = stage * half
+        held = slice(first, first + 2 * some)
+        mean_rows = slice(p * some, (p + 1) * some)
+        squares = jnp.zeros((some, 1), jnp.float32)
+        for j in range(tiles):
+            if p == 0:
+                conv_copies[j].wait()
+            cols = slice(j * COLUMN_TILE, (j + 1) * COLUMN_TILE)
+            conv_sum = jnp.dot(taps[held], conv_w[:, cols], preferred_element_type=jnp.float32)
+            here = taps[held, middle + j * COLUMN_TILE : middle + (j + 1) * COLUMN_TILE]
+            encoded = here.astype(jnp.float32) + jax.nn.gelu(conv_sum)
+            pooled = ((encoded[:some] + encoded[some:]) * 0.5).astype(jnp.bfloat16)
+            pooled_ref[mean_rows, cols] = pooled
+            wide = pooled.astype(jnp.float32)
+            squares = squares + jnp.sum(wide * wide, axis=-1, keepdims=True)
+        shrink = lax.rsqrt(squares * (1.0 / channels) + 1e-06)
+        normed = (
+            pooled_ref[mean_rows, :].astype(jnp.float32) * shrink * gain_ref[...].reshape(1, channels)
+        ).astype(jnp.bfloat16)
+        for b in range(stage):
+            outgoing[p * stage + b] = normed[b * half : (b + 1) * half]
+
+        @pl.when(jnp.logical_and(active, window // stage == p))
         def _():
-            pltpu.make_async_remote_copy(
-                src_ref=outgoing.at[to],
-                dst_ref=got.at[me],
-                send_sem=pack_send,
-                recv_sem=pack_recv,
-                device_id={"seq": target},
-                device_id_type=MESH,
-            ).start()
-
-        return carry
-
-    lax.fori_loop(0, sends, scatter, 0)
+            own.start()
+
+        def scatter(k, carry, p=p):
+            to = p * stage + lax.rem(k + mine // 2, stage)
+            target = (k // stage) * GROUP + idle + 2 * to + core
+
+            @pl.when(target != me)
+            def _():
+                pltpu.make_async_remote_copy(
+                    src_ref=outgoing.at[to],
+                    dst_ref=got.at[me],
+                    send_sem=pack_send,
+                    recv_sem=pack_recv,
+                    device_id={"seq": target},
+                    device_id_type=MESH,
+                ).start()
+
+            return carry
+
+        lax.fori_loop(0, stage * (n // GROUP), scatter, 0)
     for copy in w_copies:
         copy.wait()
 

time: 41.9 us -> 39 us (0.931)
  Pallas kernels: 37.7 us -> 34.8 us
    pallas_call x1, Pallas kernels: 37.7 us -> 34.8 us  [on_device(): pl.pallas_call(functools.partial(kernel, n, seqs, rows), out_shape=[jax.S...]
where the time goes in v3:
time: 39 us; the launch traced here: 38.8 us
  Pallas kernels  34.8 us (89%)
  local copies, waits for them, and re-layouts  3.39 us (9%)
  between operations  0.64 us (2%)
    pallas_call x1, Pallas kernels, on_device(): pl.pallas_call(functools.partial(kernel, n, seqs, rows), out_shape=[jax.S...  34.8 us
    unnamed x2, local copies, waits for them, and re-layouts  3.39 us

profile of v3, /device:TPU:31, one launch (start us, length us, event | category | flops | bytes accessed | tf_op | source)
XLA Modules:
  0.0 38.8 jit_solution(9170336121573649063)
XLA Ops:
  0.6 34.8 %shard_map.86 = (bf16[192,768]{1,0:T(8,128)(2,1)}, bf16[192,768]{1,0:T(8,128)(2,1)}) custom-call(bf16[6,64,768]{2,1,0:T(8,128)(2,1)} %x_ref.1, bf16[3840,768]{1,0:T(8,128)(2,1)} %bitcast.3, f32[768]{0:T(1024)} %gain_ref.1, bf16[768,768]{1,0:T(8,128)(2,1)} %wq_hbm.1, bf16[768,768]{1,0:T(8,128)(2,1)} %wk_hbm.1, bf16[768,768]{1,0:T(8,128)(2,1)} %wv_hbm.1, ...), custom_call_target="tpu_custom_call" | custom-call | tf_op jit(solution)/shard_map/pallas_call | solution.py:292
  35.4 1.7 %copy.11 = bf16[6,32,768]{2,1,0:T(8,128)(2,1)} copy(bf16[6,32,768]{2,1,0:T(8,128)(2,1)} %bitcast.5) | data formatting | bytes 589824
  37.1 1.7 %copy.12 = bf16[6,32,768]{2,1,0:T(8,128)(2,1)} copy(bf16[6,32,768]{2,1,0:T(8,128)(2,1)} %bitcast.4) | data formatting | bytes 589824
